TPU v7x, 32 devices: a whole 2x2x4 slice. The times are simulated.
32 devices in a mesh: group: 4 (over y, core), dev: 8 (over z, x).
Axes of the slice: x: 2, y: 2, z: 4, core: 2. Of those that a mesh axis runs over, the one named last changes fastest.
Arguments:
- node_state: bfloat16 [16384, 512], P(('group', 'dev')), may hold values from -6 to 6
- hub_state: bfloat16 [64, 512], P('dev'), may hold values from -6 to 6
- w_edge_in: bfloat16 [512, 256], replicated, may hold values from -0.25 to 0.25
- w_edge_out: bfloat16 [256, 512], replicated, may hold values from -0.375 to 0.375
- w_update: bfloat16 [512, 512], replicated, may hold values from -0.25 to 0.25
- edge_src: int32 [131072], P(('group', 'dev')), may hold values from 0 to 319
- edge_dst: int32 [131072], P(('group', 'dev')), may hold values from 0 to 319
- edge_mask: int32 [131072], P(('group', 'dev')), may hold values 0 or 1
- send_list: int32 [32, 8, 32], P(('group', 'dev')), may hold values from 0 to 511
- send_count: int32 [32, 8], P(('group', 'dev')), may hold values from 8 to 32, as said below
- node_cot: bfloat16 [16384, 512], P(('group', 'dev')), may hold values from -0.059814453 to 0.059814453
- hub_cot: bfloat16 [64, 512], P('dev'), may hold values from -0.059814453 to 0.059814453
Outputs:
- new_state: bfloat16 [16384, 512], P(('group', 'dev'))
- new_hub: bfloat16 [64, 512], P('dev')
- grad_in: float32 [512, 256], replicated
- grad_out: float32 [256, 512], replicated
- grad_update: float32 [512, 512], replicated
Inputs may be any that keep to these rules, and one draw needn't show every extreme that they name: Device 0 sends 32 live slots to peer 0: send_count[0, 0] = 32.
All inputs are finite; a program needn't handle non-finite values. No bound on the sum of `edge_mask` on one device may be relied on, other than what follows from the above.
Results may differ from a plain program's by a relative error of at most 0.0064.
The roundings to bfloat16 on the way count: a program that leaves them out, or rounds other values in their place, can miss the bound.
Values may be sent and summed in bfloat16 or wider, within the bound.
No kernel may reach another device: no remote copies, remote signals or barrier semaphores. Data moves between devices by JAX's collectives and lax.ppermute only.
A program may use at most 64 MiB of HBM per device.

v0:
```python
import jax
import jax.numpy as jnp
from jax import lax
from jax.sharding import PartitionSpec as P

F32 = jnp.float32
BF16 = jnp.bfloat16


def silu_grad(values):
    sigmoid_v = jax.nn.sigmoid(values)
    return sigmoid_v * (1.0 + values * (1.0 - sigmoid_v))


def dot(left, right, dims=((1,), (0,))):
    return lax.dot_general(left, right, (dims, ((), ())), preferred_element_type=F32)


def split_dot(left, right, dims):
    high = left.astype(BF16)
    low = (left - high.astype(F32)).astype(BF16)
    return dot(high, right, dims) + dot(low, right, dims)


def swap(blocks, axis, size, stride, total):
    position = lax.rem(lax.div(lax.axis_index(axis), stride), size)
    if size == 2:
        pairs = [(i, i ^ stride) for i in range(total)]
        other = lax.ppermute(lax.dynamic_index_in_dim(blocks, 1 - position, 0, False), axis, pairs)
        own = lax.dynamic_index_in_dim(blocks, position, 0, False)
        first = position == 0
        return jnp.stack([jnp.where(first, own, other), jnp.where(first, other, own)])
    if size * stride == total and stride == 1:
        groups = None
    else:
        groups = [
            [base + off + i * stride for i in range(size)]
            for base in range(0, total, size * stride)
            for off in range(stride)
        ]
    return lax.all_to_all(blocks, axis, 0, 0, tiled=True, axis_index_groups=groups)


def scatter_sum(value, axis, size, stride, total):
    position = lax.rem(lax.div(lax.axis_index(axis), stride), size)
    blocks = value.reshape(size, -1, value.shape[1])
    if size == 2:
        pairs = [(i, i ^ stride) for i in range(total)]
        sent = lax.dynamic_index_in_dim(blocks, 1 - position, 0, False).astype(BF16)
        own = lax.dynamic_index_in_dim(blocks, position, 0, False)
        return own + lax.ppermute(sent, axis, pairs).astype(F32)
    return jnp.sum(swap(blocks.astype(BF16), axis, size, stride, total).astype(F32), axis=0)


def gather_all(value, axis, size, stride, total):
    spread = jnp.broadcast_to(value[None], (size,) + value.shape)
    return swap(spread, axis, size, stride, total).reshape(-1, value.shape[1])


def shards(
    node_state,
    hub_state,
    w_edge_in,
    w_edge_out,
    w_update,
    edge_src,
    edge_dst,
    edge_mask,
    send_list,
    send_count,
    node_cot,
    hub_cot,
    *,
    n_group,
    n_dev
):
    width = node_state.shape[1]
    hidden_width = w_edge_in.shape[1]
    master_rows = node_state.shape[0]
    send_rows = send_list[0]
    slot_width = send_rows.shape[1]
    mirror_total = n_dev * slot_width
    hub_rows = hub_state.shape[0]
    live_slot = jnp.arange(slot_width)[None, :] < send_count[0][:, None]
    chosen = jnp.where(live_slot, send_rows, -1).reshape(1, -1)
    select = (jnp.arange(master_rows)[:, None] == chosen).astype(BF16)
    outgoing = dot(select, node_state, ((0,), (0,))).astype(BF16)
    packed = jnp.concatenate(
        [
            outgoing.reshape(n_dev, slot_width, width),
            jnp.broadcast_to(hub_state[None], (n_dev, hub_rows, width)),
        ],
        axis=1,
    )
    arrived = lax.all_to_all(packed, "dev", 0, 0, tiled=True)
    table = jnp.concatenate(
        [
            arrived[:, :slot_width].reshape(mirror_total, width),
            arrived[:, slot_width:].reshape(-1, width),
        ],
        axis=0,
    )
    local_rows = table.shape[0]
    ids = jnp.arange(local_rows)[:, None]
    from_hot = (ids == edge_src[None, :]).astype(BF16)
    to_hot = (ids == jnp.where(edge_mask > 0, edge_dst, -1)[None, :]).astype(BF16)
    adjacency = dot(to_hot, from_hot, ((1,), (1,)))
    adj_high = jnp.floor(adjacency * (1.0 / 256.0))
    adj_low = (adjacency - 256.0 * adj_high).astype(BF16)
    adj_high = adj_high.astype(BF16)
    counts = jnp.sum(adjacency, axis=1)
    pre_act = dot(table, w_edge_in)
    hidden = jax.nn.silu(pre_act).astype(BF16)
    partial = dot(adj_low, hidden) + 256.0 * dot(adj_high, hidden)

    def by_peer(value, hubs_of):
        return jnp.concatenate(
            [
                value[:mirror_total].reshape((n_dev, slot_width) + value.shape[1:]),
                value[mirror_total:].reshape((n_dev, hubs_of) + value.shape[1:]),
            ],
            axis=1,
        )

    rounded_count = counts.astype(BF16)
    rest_count = (counts - rounded_count.astype(F32)).astype(BF16)
    count_rows = jnp.stack(
        [by_peer(rounded_count, hub_rows), by_peer(rest_count, hub_rows)], axis=1
    )
    count_rows = jnp.pad(count_rows, ((0, 0), (0, 6), (0, hidden_width - slot_width - hub_rows)))
    message = jnp.concatenate([by_peer(partial.astype(BF16), hub_rows), count_rows], axis=1)
    back = lax.all_to_all(message, "dev", 0, 0, tiled=True)
    base = slot_width + hub_rows
    back_part = back[:, :slot_width].reshape(mirror_total, hidden_width)
    back_count = back[:, base, :slot_width].reshape(mirror_total, 1)
    summed_hidden = dot(select, back_part)
    degree = dot(select, back_count)
    hub_hidden = jnp.sum(back[:, slot_width:base].astype(F32), axis=0)
    hub_degree = jnp.sum(back[:, base : base + 2, slot_width:base].astype(F32), axis=(0, 1))
    hub_sums = jnp.concatenate(
        [hub_hidden, jnp.broadcast_to(hub_degree[:, None], (hub_rows, 128))], axis=1
    )
    hub_sums = lax.psum(hub_sums, "group")
    hub_hidden, hub_degree = (
        hub_sums[:, :hidden_width],
        hub_sums[:, hidden_width : hidden_width + 1],
    )
    states = jnp.concatenate([node_state, hub_state], axis=0).astype(F32)
    cotangent = jnp.concatenate([node_cot, hub_cot], axis=0).astype(F32)
    degree = jnp.maximum(jnp.concatenate([degree, hub_degree], axis=0), 1.0)
    summed_hidden = jnp.concatenate([summed_hidden, hub_hidden], axis=0)
    summed = split_dot(summed_hidden, w_edge_out, ((1,), (0,)))
    mixed = (states + summed / degree).astype(BF16)
    pre_update = dot(mixed, w_update)
    updated = (states + jax.nn.silu(pre_update)).astype(BF16)
    grad_pre = (cotangent * silu_grad(pre_update)).astype(BF16)
    grad_sum = (dot(grad_pre, w_update, ((1,), (1,))) / degree).astype(BF16)
    grad_hidden = dot(grad_sum, w_edge_out, ((1,), (1,))).astype(BF16)
    grad_outgoing = dot(select, grad_hidden[:master_rows], ((0,), (0,))).astype(BF16)
    packed_grad = jnp.concatenate(
        [
            grad_outgoing.reshape(n_dev, slot_width, hidden_width),
            jnp.broadcast_to(grad_hidden[None, master_rows:], (n_dev, hub_rows, hidden_width)),
        ],
        axis=1,
    )
    arrived_grad = lax.all_to_all(packed_grad, "dev", 0, 0, tiled=True)
    grad_rows = jnp.concatenate(
        [
            arrived_grad[:, :slot_width].reshape(mirror_total, hidden_width),
            arrived_grad[:, slot_width:].reshape(-1, hidden_width),
        ],
        axis=0,
    )
    row_weight = jnp.where(
        jnp.arange(mixed.shape[0])[:, None] < master_rows,
        1.0,
        (lax.axis_index("group") == 0).astype(F32),
    )
    weighted = (grad_pre.astype(F32) * row_weight).astype(BF16)
    grad_update = dot(mixed, weighted, ((0,), (0,)))
    grad_out = split_dot(summed_hidden * row_weight, grad_sum, ((0,), (0,)))
    by_source = dot(adj_low, grad_rows, ((0,), (0,))) + 256.0 * dot(
        adj_high, grad_rows, ((0,), (0,))
    )
    grad_act = by_source * silu_grad(pre_act)
    act_high = grad_act.astype(BF16)
    act_low = (grad_act - act_high.astype(F32)).astype(BF16)
    grad_in = dot(table, act_high, ((0,), (0,))) + dot(table, act_low, ((0,), (0,)))
    half = width // 2
    side = jnp.concatenate([grad_in[:half], grad_in[half:]], axis=1)
    whole = jnp.concatenate([grad_update, grad_out, side], axis=0)
    whole = scatter_sum(whole, "group", 2, 1, n_group)
    whole = scatter_sum(whole, "group", n_group // 2, 2, n_group)
    whole = scatter_sum(whole, "dev", n_dev, 1, n_dev)
    whole = gather_all(whole.astype(BF16), "dev", n_dev, 1, n_dev)
    whole = gather_all(whole, "group", n_group // 2, 2, n_group)
    whole = gather_all(whole, "group", 2, 1, n_group).astype(F32)
    side = whole[width + hidden_width :]
    return (
        updated[:master_rows],
        updated[master_rows:],
        jnp.concatenate([side[:, :hidden_width], side[:, hidden_width:]], axis=0),
        whole[width : width + hidden_width],
        whole[:width],
    )


def solution(mesh):

    def body(*args):
        return shards(*args, n_group=mesh.shape["group"], n_dev=mesh.shape["dev"])

    return jax.shard_map(
        body,
        mesh=mesh,
        in_specs=(
            P(("group", "dev"), None),
            P("dev", None),
            P(),
            P(),
            P(),
            P(("group", "dev")),
            P(("group", "dev")),
            P(("group", "dev")),
            P(("group", "dev"), None, None),
            P(("group", "dev"), None),
            P(("group", "dev"), None),
            P("dev", None),
        ),
        out_specs=(P(("group", "dev"), None), P("dev", None), P(), P(), P()),
        check_vma=False,
    )
```

profile of v0, /device:TPU:0, one launch (start us, length us, event | category | flops | bytes accessed | tf_op | source)
XLA Modules:
  0.0 114.2 jit_solution(3356900994865378915)
XLA Ops:
  0.6 0.8 iota_compare_fusion.11
  1.5 0.8 squeeze.19
  2.3 1.4 %convolution_convert_fusion.1 = bf16[256,512]{1,0:T(8,128)(2,1)S(1)} fusion(bf16[512,512]{1,0:T(8,128)(2,1)} %param.12, s32[256]{0:T(256)S(1)} %broadcast_select_fusion), kind=kOutput, calls=%fused_computation.16 | convolution fusion | flops 134479872 | bytes 787456 | tf_op jit(solution)/shard_map/dot_general | solution.py:16
  3.7 0.7 broadcast_in_dim.28
  4.4 0.7 pad_maximum_fusion.4
  5.2 7.3 %all-to-all-start = ((bf16[8,40,512]{2,1,0:T(8,128)(2,1)}), bf16[8,40,512]{2,1,0:T(8,128)(2,1)S(1)}, u32[]{:S(2)}, u32[]{:S(2)}) async-start(bf16[8,40,512]{2,1,0:T(8,128)(2,1)} %pad_maximum_fusion.4), calls=%async_computation | async-start | bytes 655360 | tf_op jit(solution)/shard_map/all_to_all | solution.py:95
  12.5 2.0 %fusion.62 = (f32[320]{0:T(512)S(1)}, f32[320,320]{0,1:T(8,128)S(1)}) fusion(s32[4096]{0:T(1024)S(1)} %copy-done.13, s32[4096]{0:T(1024)S(1)} %compare_select_fusion), kind=kOutput, calls=%fused_computation.120 | convolution fusion | flops 841584320 | bytes 443648 | tf_op jit(solution)/shard_map/dot_general | solution.py:16
  14.8 8.0 %all-to-all-done = bf16[8,40,512]{2,1,0:T(8,128)(2,1)S(1)} async-done(((bf16[8,40,512]{2,1,0:T(8,128)(2,1)}), bf16[8,40,512]{2,1,0:T(8,128)(2,1)S(1)}, u32[]{:S(2)}, u32[]{:S(2)}) %all-to-all-start) | async-done | bytes 327712 | tf_op jit(solution)/shard_map/all_to_all | solution.py:95
  23.8 0.7 fusion.33
  24.5 3.6 %all-to-all-start.1 = ((bf16[8,48,256]{2,1,0:T(8,128)(2,1)}), bf16[8,48,256]{2,1,0:T(8,128)(2,1)S(1)}, u32[]{:S(2)}, u32[]{:S(2)}) async-start(bf16[8,48,256]{2,1,0:T(8,128)(2,1)} %fusion.33), calls=%async_computation.1 | async-start | bytes 393216 | tf_op jit(solution)/shard_map/all_to_all | solution.py:132
  28.1 7.8 %all-to-all-done.1 = bf16[8,48,256]{2,1,0:T(8,128)(2,1)S(1)} async-done(((bf16[8,48,256]{2,1,0:T(8,128)(2,1)}), bf16[8,48,256]{2,1,0:T(8,128)(2,1)S(1)}, u32[]{:S(2)}, u32[]{:S(2)}) %all-to-all-start.1) | async-done | bytes 196640 | tf_op jit(solution)/shard_map/all_to_all | solution.py:132
  36.0 10.1 %psum.7 = f32[8,384]{1,0:T(8,128)S(1)} all-reduce(f32[8,384]{1,0:T(8,128)S(1)} %pad_maximum_fusion.16), channel_id=1, replica_groups=mesh['group'=4,'dev'=8] {'group'}, use_global_device_ids=true, to_apply=%region_3.4 | all-reduce | flops 3072 | bytes 24576 | tf_op jit(solution)/shard_map/psum | solution.py:143
  48.6 1.7 %multiply_convert_fusion.1 = (bf16[520,512]{1,0:T(8,128)(2,1)S(1)}, bf16[520,512]{1,0:T(8,128)(2,1)}) fusion(bf16[8,512]{1,0:T(8,128)(2,1)S(1)} %copy-done.14, bf16[512,512]{1,0:T(8,128)(2,1)S(1)} %copy-done.11, bf16[8,512]{1,0:T(8,128)(2,1)S(1)} %copy-done.10, bf16[512,512]{1,0:T(8,128)(2,1)S(1)} %copy-done.12, bf16[520,512]{1,0:T(8,128)(2,1)S(1)} %fusion.5, ...), kind=kOutput, calls=%fused_computation.26 | convolution fusion | flops 277954560 | bytes 3186688 | tf_op jit(solution)/shard_map/dot_general | solution.py:16
  51.8 0.7 pad_maximum_fusion.9
  52.5 3.4 %all-to-all-start.2 = ((bf16[8,40,256]{2,1,0:T(8,128)(2,1)}), bf16[8,40,256]{2,1,0:T(8,128)(2,1)S(1)}, u32[]{:S(2)}, u32[]{:S(2)}) async-start(bf16[8,40,256]{2,1,0:T(8,128)(2,1)} %pad_maximum_fusion.9), calls=%async_computation.2 | async-start | bytes 327680 | tf_op jit(solution)/shard_map/all_to_all | solution.py:167
  57.7 1.7 %fusion.12 = f32[512,512]{1,0:T(8,128)} fusion(bf16[520,512]{1,0:T(8,128)(2,1)S(1)} %copy-done.16, bf16[520,512]{1,0:T(8,128)(2,1)S(1)} %copy-done.18, f32[520]{0:T(1024)S(1)} %fusion.44), kind=kOutput, calls=%fused_computation.32 | convolution fusion | flops 273428480 | bytes 2115616 | tf_op jit(solution)/shard_map/dot_general | solution.py:16
  59.3 4.1 %all-to-all-done.2 = bf16[8,40,256]{2,1,0:T(8,128)(2,1)S(1)} async-done(((bf16[8,40,256]{2,1,0:T(8,128)(2,1)}), bf16[8,40,256]{2,1,0:T(8,128)(2,1)S(1)}, u32[]{:S(2)}, u32[]{:S(2)}) %all-to-all-start.2) | async-done | bytes 163872 | tf_op jit(solution)/shard_map/all_to_all | solution.py:167
  64.7 0.8 copy-done.3
  65.9 2.0 %collective-permute-done = bf16[512,512]{1,0:T(8,128)(2,1)} collective-permute-done((bf16[512,512]{1,0:T(8,128)(2,1)S(1)}, bf16[512,512]{1,0:T(8,128)(2,1)}, u32[]{:S(2)}, u32[]{:S(2)}) %collective-permute-start) | collective-permute-done | bytes 524320 | tf_op jit(solution)/shard_map/ppermute | solution.py:51
  67.9 1.2 %bitcast_add_fusion = f32[512,512]{1,0:T(8,128)S(1)} fusion(bf16[512,512]{1,0:T(8,128)(2,1)} %collective-permute-done, f32[2,512,512]{2,1,0:T(8,128)S(1)} %bitcast.66, s32[]{:T(128)S(6)} %select_n.70), kind=kLoop, calls=%fused_computation.30 | loop fusion | flops 524288 | bytes 2621444 | tf_op jit(solution)/shard_map/add | solution.py:51
  69.1 1.0 copy-done.1
  70.1 1.6 %collective-permute-start.1 = (bf16[256,512]{1,0:T(8,128)(2,1)S(1)}, bf16[256,512]{1,0:T(8,128)(2,1)S(1)}, u32[]{:S(2)}, u32[]{:S(2)}) collective-permute-start(bf16[256,512]{1,0:T(8,128)(2,1)S(1)} %fusion.23), channel_id=1, source_target_pairs={{0,16},{8,24},{16,0},{24,8},{1,17},{9,25},{17,1},{25,9},{2,18},{10... | collective-permute-start | bytes 786440 | tf_op jit(solution)/shard_map/ppermute | solution.py:51
  71.7 6.8 %collective-permute-done.1 = bf16[256,512]{1,0:T(8,128)(2,1)S(1)} collective-permute-done((bf16[256,512]{1,0:T(8,128)(2,1)S(1)}, bf16[256,512]{1,0:T(8,128)(2,1)S(1)}, u32[]{:S(2)}, u32[]{:S(2)}) %collective-permute-start.1) | collective-permute-done | bytes 262176 | tf_op jit(solution)/shard_map/ppermute | solution.py:51
  78.6 1.1 fusion.15
  79.7 11.1 %all_to_all.25 = bf16[8,32,512]{2,1,0:T(8,128)(2,1)S(1)} all-to-all(bf16[8,32,512]{2,1,0:T(8,128)(2,1)S(1)} %bitcast.74), channel_id=1, replica_groups=mesh['group'=4,'dev'=8] {'dev'}, dimensions={0} | all-to-all | bytes 524288 | tf_op jit(solution)/shard_map/all_to_all | solution.py:41
  90.8 11.9 %all_to_all.26 = bf16[8,32,512]{2,1,0:T(8,128)(2,1)S(1)} all-to-all(bf16[8,32,512]{2,1,0:T(8,128)(2,1)S(1)} %broadcast_in_dim.32), channel_id=1, replica_groups=mesh['group'=4,'dev'=8] {'dev'}, dimensions={0} | all-to-all | bytes 524288 | tf_op jit(solution)/shard_map/all_to_all | solution.py:41
  102.7 1.5 %collective-permute-start.2 = (bf16[256,512]{1,0:T(8,128)(2,1)S(1)}, bf16[256,512]{1,0:T(8,128)(2,1)S(1)}, u32[]{:S(2)}, u32[]{:S(2)}) collective-permute-start(bf16[256,512]{1,0:T(8,128)(2,1)S(1)} %bitcast.73), channel_id=1, source_target_pairs={{0,16},{8,24},{16,0},{24,8},{1,17},{9,25},{17,1},{25,9},{2,18},{10... | collective-permute-start | bytes 786440 | tf_op jit(solution)/shard_map/ppermute | solution.py:29
  104.3 4.8 %collective-permute-done.2 = bf16[256,512]{1,0:T(8,128)(2,1)S(1)} collective-permute-done((bf16[256,512]{1,0:T(8,128)(2,1)S(1)}, bf16[256,512]{1,0:T(8,128)(2,1)S(1)}, u32[]{:S(2)}, u32[]{:S(2)}) %collective-permute-start.2) | collective-permute-done | bytes 262176 | tf_op jit(solution)/shard_map/ppermute | solution.py:29
  109.3 0.8 slice.131
  111.5 0.8 slice.141
  112.3 1.0 slice_bitcast_fusion
  113.4 0.8 pad_maximum_fusion.3
  (100 shorter events, 10.4 us)
Async XLA Ops:
  0.6 47.3 %copy-start = (bf16[512,512]{1,0:T(8,128)(2,1)S(1)}, bf16[512,512]{1,0:T(8,128)(2,1)}, u32[]{:S(2)}) copy-start(bf16[512,512]{1,0:T(8,128)(2,1)} %param.16) | copy-start | bytes 1572868
  2.3 10.2 %copy-start.8 = (s32[4096]{0:T(1024)S(1)}, s32[4096]{0:T(1024)}, u32[]{:S(2)}) copy-start(s32[4096]{0:T(1024)} %param.18) | copy-start | bytes 49156
  2.3 10.2 %copy-start.9 = (s32[4096]{0:T(1024)S(1)}, s32[4096]{0:T(1024)}, u32[]{:S(2)}) copy-start(s32[4096]{0:T(1024)} %param.19) | copy-start | bytes 49156
  2.3 10.2 %copy-start.13 = (s32[4096]{0:T(1024)S(1)}, s32[4096]{0:T(1024)}, u32[]{:S(2)}) copy-start(s32[4096]{0:T(1024)} %param.17) | copy-start | bytes 49156
  5.2 17.6 %all-to-all-start = ((bf16[8,40,512]{2,1,0:T(8,128)(2,1)}), bf16[8,40,512]{2,1,0:T(8,128)(2,1)S(1)}, u32[]{:S(2)}, u32[]{:S(2)}) async-start(bf16[8,40,512]{2,1,0:T(8,128)(2,1)} %pad_maximum_fusion.4), calls=%async_computation | async-start | bytes 655360 | tf_op jit(solution)/shard_map/all_to_all | solution.py:95
  12.5 10.3 %copy-start.7 = (bf16[512,256]{1,0:T(8,128)(2,1)S(1)}, bf16[512,256]{1,0:T(8,128)(2,1)}, u32[]{:S(2)}) copy-start(bf16[512,256]{1,0:T(8,128)(2,1)} %param.14) | copy-start | bytes 786436
  14.5 8.9 %copy-start.5 = (f32[320,320]{0,1:T(8,128)}, f32[320,320]{0,1:T(8,128)S(1)}, u32[]{:S(2)}) copy-start(f32[320,320]{0,1:T(8,128)S(1)} %get-tuple-element.16) | copy-start | bytes 1228804
  23.8 23.1 %copy-start.2 = (bf16[256,512]{1,0:T(8,128)(2,1)S(1)}, bf16[256,512]{1,0:T(8,128)(2,1)}, u32[]{:S(2)}) copy-start(bf16[256,512]{1,0:T(8,128)(2,1)} %param.15) | copy-start | bytes 786436
  24.5 11.4 %all-to-all-start.1 = ((bf16[8,48,256]{2,1,0:T(8,128)(2,1)}), bf16[8,48,256]{2,1,0:T(8,128)(2,1)S(1)}, u32[]{:S(2)}, u32[]{:S(2)}) async-start(bf16[8,48,256]{2,1,0:T(8,128)(2,1)} %fusion.33), calls=%async_computation.1 | async-start | bytes 393216 | tf_op jit(solution)/shard_map/all_to_all | solution.py:132
  46.5 0.7 copy-start.10
  46.5 1.1 copy-start.12
  47.6 1.0 copy-start.11
  47.6 1.0 copy-start.14
  48.6 1.7 %copy-start.15 = (bf16[520,512]{1,0:T(8,128)(2,1)}, bf16[520,512]{1,0:T(8,128)(2,1)S(1)}, u32[]{:S(2)}) copy-start(bf16[520,512]{1,0:T(8,128)(2,1)S(1)} %fusion.5) | copy-start | bytes 1597444
  50.3 0.8 copy-start.17
  52.5 10.9 %all-to-all-start.2 = ((bf16[8,40,256]{2,1,0:T(8,128)(2,1)}), bf16[8,40,256]{2,1,0:T(8,128)(2,1)S(1)}, u32[]{:S(2)}, u32[]{:S(2)}) async-start(bf16[8,40,256]{2,1,0:T(8,128)(2,1)} %pad_maximum_fusion.9), calls=%async_computation.2 | async-start | bytes 327680 | tf_op jit(solution)/shard_map/all_to_all | solution.py:167
  56.5 1.1 copy-start.16
  56.5 1.2 %copy-start.18 = (bf16[520,512]{1,0:T(8,128)(2,1)S(1)}, bf16[520,512]{1,0:T(8,128)(2,1)}, u32[]{:S(2)}) copy-start(bf16[520,512]{1,0:T(8,128)(2,1)} %copy-done.17) | copy-start | bytes 1597444
  57.7 5.8 %copy-start.6 = (f32[320,320]{0,1:T(8,128)S(1)}, f32[320,320]{0,1:T(8,128)}, u32[]{:S(2)}) copy-start(f32[320,320]{0,1:T(8,128)} %copy-done.5) | copy-start | bytes 1228804
  64.3 1.2 %copy-start.3 = (f32[512,512]{1,0:T(8,128)S(1)}, f32[512,512]{1,0:T(8,128)}, u32[]{:S(2)}) copy-start(f32[512,512]{1,0:T(8,128)} %fusion.12) | copy-start | bytes 3145732
  65.8 2.1 %collective-permute-start = (bf16[512,512]{1,0:T(8,128)(2,1)S(1)}, bf16[512,512]{1,0:T(8,128)(2,1)}, u32[]{:S(2)}, u32[]{:S(2)}) collective-permute-start(bf16[512,512]{1,0:T(8,128)(2,1)S(1)} %fusion.14), channel_id=1, source_target_pairs={{0,8},{8,0},{16,24},{24,16},{1,9},{9,1},{17,25},{25,17},{2,10},{10... | collective-permute-start | bytes 1572872 | tf_op jit(solution)/shard_map/ppermute | solution.py:51
  69.1 1.0 copy-start.1
  70.1 8.4 %collective-permute-start.1 = (bf16[256,512]{1,0:T(8,128)(2,1)S(1)}, bf16[256,512]{1,0:T(8,128)(2,1)S(1)}, u32[]{:S(2)}, u32[]{:S(2)}) collective-permute-start(bf16[256,512]{1,0:T(8,128)(2,1)S(1)} %fusion.23), channel_id=1, source_target_pairs={{0,16},{8,24},{16,0},{24,8},{1,17},{9,25},{17,1},{25,9},{2,18},{10... | collective-permute-start | bytes 786440 | tf_op jit(solution)/shard_map/ppermute | solution.py:51
  102.7 6.6 %copy-start.4 = (bf16[520,512]{1,0:T(8,128)(2,1)S(1)}, bf16[520,512]{1,0:T(8,128)(2,1)}, u32[]{:S(2)}) copy-start(bf16[520,512]{1,0:T(8,128)(2,1)} %get-tuple-element.8) | copy-start | bytes 1597444
  102.7 6.4 %collective-permute-start.2 = (bf16[256,512]{1,0:T(8,128)(2,1)S(1)}, bf16[256,512]{1,0:T(8,128)(2,1)S(1)}, u32[]{:S(2)}, u32[]{:S(2)}) collective-permute-start(bf16[256,512]{1,0:T(8,128)(2,1)S(1)} %bitcast.73), channel_id=1, source_target_pairs={{0,16},{8,24},{16,0},{24,8},{1,17},{9,25},{17,1},{25,9},{2,18},{10... | collective-permute-start | bytes 786440 | tf_op jit(solution)/shard_map/ppermute | solution.py:29
  109.2 2.0 %collective-permute-start.3 = (bf16[512,512]{1,0:T(8,128)(2,1)S(1)}, bf16[512,512]{1,0:T(8,128)(2,1)S(1)}, u32[]{:S(2)}, u32[]{:S(2)}) collective-permute-start(bf16[512,512]{1,0:T(8,128)(2,1)S(1)} %bitcast.72), channel_id=1, source_target_pairs={{0,8},{8,0},{16,24},{24,16},{1,9},{9,1},{17,25},{25,17},{2,10},{10... | collective-permute-start | bytes 1572872 | tf_op jit(solution)/shard_map/ppermute | solution.py:29
where the time goes:
time: 115 us; the launch traced here: 114 us
  waiting for transfers between devices  33.9 us (29%)
  blocking collectives  33.1 us (29%)
  starting transfers between devices  17.5 us (15%)
  matrix products  12.1 us (11%)
  local copies, waits for them, and re-layouts  9.5 us (8%)
  other arithmetic  6.87 us (6%)
    all_to_all x2, blocking collectives, swap(): lax.all_to_all(blocks, axis, 0, 0, tiled=True, axis_index_groups=groups)  23 us
    dot_general x20, matrix products, dot(): lax.dot_general(left, right, (dims, ((), ())), preferred_element_type=F32)  12.1 us
    psum x1, blocking collectives, shards(): hub_sums = lax.psum(hub_sums, 'group')  10.1 us
    ppermute x2, waiting for transfers between devices, scatter_sum(): return own + lax.ppermute(sent, axis, pairs).astype(F32)  8.81 us
    all_to_all x1, waiting for transfers between devices, shards(): arrived = lax.all_to_all(packed, 'dev', 0, 0, tiled=True)  7.98 us
    all_to_all x1, waiting for transfers between devices, shards(): back = lax.all_to_all(message, 'dev', 0, 0, tiled=True)  7.78 us
    all_to_all x1, starting transfers between devices, shards(): arrived = lax.all_to_all(packed, 'dev', 0, 0, tiled=True)  7.25 us
    ppermute x2, waiting for transfers between devices, swap(): lax.ppermute(lax.dynamic_index_in_dim(blocks, 1 - position, 0, False), ax...  5.28 us
  transfers between devices with their start and end apart: 7, of which 7 were waited for; matrix products, arithmetic and copies ran while one was open for 6% of the time, Pallas kernels for 0%

commit v1 on v0

--- a/solution.py
+++ b/solution.py
@@ -140,7 +140,11 @@
     hub_sums = jnp.concatenate(
         [hub_hidden, jnp.broadcast_to(hub_degree[:, None], (hub_rows, 128))], axis=1
     )
-    hub_sums = lax.psum(hub_sums, "group")
+    hub_sums = hub_sums
+    for hop in (1, 2):
+        hub_sums = hub_sums + lax.ppermute(
+            hub_sums, "group", [(dev, dev ^ hop) for dev in range(4)]
+        )
     hub_hidden, hub_degree = (
         hub_sums[:, :hidden_width],
         hub_sums[:, hidden_width : hidden_width + 1],

time: 115 us -> 109 us (0.948)
  blocking collectives: 33.1 us -> 23 us
  waiting for transfers between devices: 33.9 us -> 36.7 us
  starting transfers between devices: 17.5 us -> 19 us
    psum x1 -> x0, blocking collectives: 10.1 us -> none  [shards(): hub_sums = lax.psum(hub_sums, 'group')]
    ppermute x0 -> x2, waiting for transfers between devices: none -> 2.74 us  [shards(): lax.ppermute(hub_sums, 'group', [(dev, dev ^ hop) for dev in range(4)])]
    ppermute x0 -> x2, starting transfers between devices: none -> 1.54 us  [shards(): lax.ppermute(hub_sums, 'group', [(dev, dev ^ hop) for dev in range(4)])]
  transfers between devices with their start and end apart: 7 -> 9, of which waited for: 7 -> 9; matrix products, arithmetic and copies ran while one was open for 6% -> 6% of each run, Pallas kernels for 0% -> 0%
where the time goes in v1:
time: 109 us; the launch traced here: 108 us
  waiting for transfers between devices  36.7 us (34%)
  blocking collectives  23 us (21%)
  starting transfers between devices  19 us (17%)
  matrix products  12.2 us (11%)
  local copies, waits for them, and re-layouts  9.08 us (8%)
  other arithmetic  6.88 us (6%)
  between operations  1.19 us (1%)
    all_to_all x2, blocking collectives, swap(): lax.all_to_all(blocks, axis, 0, 0, tiled=True, axis_index_groups=groups)  23 us
    dot_general x20, matrix products, dot(): lax.dot_general(left, right, (dims, ((), ())), preferred_element_type=F32)  12.2 us
    ppermute x2, waiting for transfers between devices, scatter_sum(): return own + lax.ppermute(sent, axis, pairs).astype(F32)  8.84 us
    all_to_all x1, waiting for transfers between devices, shards(): arrived = lax.all_to_all(packed, 'dev', 0, 0, tiled=True)  7.98 us
    all_to_all x1, waiting for transfers between devices, shards(): back = lax.all_to_all(message, 'dev', 0, 0, tiled=True)  7.78 us
    all_to_all x1, starting transfers between devices, shards(): arrived = lax.all_to_all(packed, 'dev', 0, 0, tiled=True)  7.25 us
    ppermute x2, waiting for transfers between devices, swap(): lax.ppermute(lax.dynamic_index_in_dim(blocks, 1 - position, 0, False), ax...  5.31 us
    all_to_all x1, waiting for transfers between devices, shards(): arrived_grad = lax.all_to_all(packed_grad, 'dev', 0, 0, tiled=True)  4.07 us
  transfers between devices with their start and end apart: 9, of which 9 were waited for; matrix products, arithmetic and copies ran while one was open for 6% of the time, Pallas kernels for 0%

profile of v1, /device:TPU:0, one launch (start us, length us, event | category | flops | bytes accessed | tf_op | source)
XLA Modules:
  0.0 108.0 jit_solution(12380594611761334332)
XLA Ops:
  0.6 0.8 iota_compare_fusion.11
  1.5 0.8 squeeze.19
  2.3 1.4 %convolution_convert_fusion.1 = bf16[256,512]{1,0:T(8,128)(2,1)S(1)} fusion(bf16[512,512]{1,0:T(8,128)(2,1)} %param.12, s32[256]{0:T(256)S(1)} %broadcast_select_fusion), kind=kOutput, calls=%fused_computation.16 | convolution fusion | flops 134479872 | bytes 787456 | tf_op jit(solution)/shard_map/dot_general | solution.py:16
  3.7 0.7 broadcast_in_dim.28
  4.4 0.7 pad_maximum_fusion.4
  5.2 7.3 %all-to-all-start = ((bf16[8,40,512]{2,1,0:T(8,128)(2,1)}), bf16[8,40,512]{2,1,0:T(8,128)(2,1)S(1)}, u32[]{:S(2)}, u32[]{:S(2)}) async-start(bf16[8,40,512]{2,1,0:T(8,128)(2,1)} %pad_maximum_fusion.4), calls=%async_computation | async-start | bytes 655360 | tf_op jit(solution)/shard_map/all_to_all | solution.py:95
  12.5 2.0 %fusion.63 = (f32[320]{0:T(512)S(1)}, f32[320,320]{0,1:T(8,128)S(1)}) fusion(s32[4096]{0:T(1024)S(1)} %copy-done.13, s32[4096]{0:T(1024)S(1)} %compare_select_fusion), kind=kOutput, calls=%fused_computation.121 | convolution fusion | flops 841584320 | bytes 443648 | tf_op jit(solution)/shard_map/dot_general | solution.py:16
  14.8 8.0 %all-to-all-done = bf16[8,40,512]{2,1,0:T(8,128)(2,1)S(1)} async-done(((bf16[8,40,512]{2,1,0:T(8,128)(2,1)}), bf16[8,40,512]{2,1,0:T(8,128)(2,1)S(1)}, u32[]{:S(2)}, u32[]{:S(2)}) %all-to-all-start) | async-done | bytes 327712 | tf_op jit(solution)/shard_map/all_to_all | solution.py:95
  24.5 3.6 %all-to-all-start.1 = ((bf16[8,48,256]{2,1,0:T(8,128)(2,1)}), bf16[8,48,256]{2,1,0:T(8,128)(2,1)S(1)}, u32[]{:S(2)}, u32[]{:S(2)}) async-start(bf16[8,48,256]{2,1,0:T(8,128)(2,1)} %fusion.33), calls=%async_computation.1 | async-start | bytes 393216 | tf_op jit(solution)/shard_map/all_to_all | solution.py:132
  28.1 7.8 %all-to-all-done.1 = bf16[8,48,256]{2,1,0:T(8,128)(2,1)S(1)} async-done(((bf16[8,48,256]{2,1,0:T(8,128)(2,1)}), bf16[8,48,256]{2,1,0:T(8,128)(2,1)S(1)}, u32[]{:S(2)}, u32[]{:S(2)}) %all-to-all-start.1) | async-done | bytes 196640 | tf_op jit(solution)/shard_map/all_to_all | solution.py:132
  36.5 0.8 collective-permute-done
  37.2 1.5 %collective-permute-start.1 = (f32[8,384]{1,0:T(8,128)S(1)}, f32[8,384]{1,0:T(8,128)S(1)}, u32[]{:S(2)}, u32[]{:S(2)}) collective-permute-start(f32[8,384]{1,0:T(8,128)S(1)} %fusion.60), channel_id=1, source_target_pairs={{0,16},{8,24},{16,0},{24,8},{1,17},{9,25},{17,1},{25,9},{2,18},{10... | collective-permute-start | bytes 36872 | tf_op jit(solution)/shard_map/ppermute | solution.py:145
  39.0 2.0 %collective-permute-done.1 = f32[8,384]{1,0:T(8,128)S(1)} collective-permute-done((f32[8,384]{1,0:T(8,128)S(1)}, f32[8,384]{1,0:T(8,128)S(1)}, u32[]{:S(2)}, u32[]{:S(2)}) %collective-permute-start.1) | collective-permute-done | bytes 12320 | tf_op jit(solution)/shard_map/ppermute | solution.py:145
  42.4 1.7 %multiply_convert_fusion.1 = (bf16[520,512]{1,0:T(8,128)(2,1)S(1)}, bf16[520,512]{1,0:T(8,128)(2,1)}) fusion(bf16[8,512]{1,0:T(8,128)(2,1)S(1)} %copy-done.14, bf16[512,512]{1,0:T(8,128)(2,1)S(1)} %copy-done.11, bf16[8,512]{1,0:T(8,128)(2,1)S(1)} %copy-done.10, bf16[512,512]{1,0:T(8,128)(2,1)S(1)} %copy-done.12, bf16[520,512]{1,0:T(8,128)(2,1)S(1)} %fusion.5, ...), kind=kOutput, calls=%fused_computation.26 | convolution fusion | flops 277954560 | bytes 3186688 | tf_op jit(solution)/shard_map/dot_general | solution.py:16
  46.3 3.4 %all-to-all-start.2 = ((bf16[8,40,256]{2,1,0:T(8,128)(2,1)}), bf16[8,40,256]{2,1,0:T(8,128)(2,1)S(1)}, u32[]{:S(2)}, u32[]{:S(2)}) async-start(bf16[8,40,256]{2,1,0:T(8,128)(2,1)} %pad_maximum_fusion.9), calls=%async_computation.2 | async-start | bytes 327680 | tf_op jit(solution)/shard_map/all_to_all | solution.py:171
  51.5 1.7 %fusion.12 = f32[512,512]{1,0:T(8,128)} fusion(bf16[520,512]{1,0:T(8,128)(2,1)S(1)} %copy-done.16, bf16[520,512]{1,0:T(8,128)(2,1)S(1)} %copy-done.18, f32[520]{0:T(1024)S(1)} %fusion.44), kind=kOutput, calls=%fused_computation.32 | convolution fusion | flops 273428480 | bytes 2115616 | tf_op jit(solution)/shard_map/dot_general | solution.py:16
  53.2 4.1 %all-to-all-done.2 = bf16[8,40,256]{2,1,0:T(8,128)(2,1)S(1)} async-done(((bf16[8,40,256]{2,1,0:T(8,128)(2,1)}), bf16[8,40,256]{2,1,0:T(8,128)(2,1)S(1)}, u32[]{:S(2)}, u32[]{:S(2)}) %all-to-all-start.2) | async-done | bytes 163872 | tf_op jit(solution)/shard_map/all_to_all | solution.py:171
  58.5 0.8 copy-done.3
  59.7 2.0 %collective-permute-done.2 = bf16[512,512]{1,0:T(8,128)(2,1)} collective-permute-done((bf16[512,512]{1,0:T(8,128)(2,1)S(1)}, bf16[512,512]{1,0:T(8,128)(2,1)}, u32[]{:S(2)}, u32[]{:S(2)}) %collective-permute-start.2) | collective-permute-done | bytes 524320 | tf_op jit(solution)/shard_map/ppermute | solution.py:51
  61.8 1.2 %bitcast_add_fusion = f32[512,512]{1,0:T(8,128)S(1)} fusion(bf16[512,512]{1,0:T(8,128)(2,1)} %collective-permute-done.2, f32[2,512,512]{2,1,0:T(8,128)S(1)} %bitcast.66, s32[]{:T(128)S(6)} %select_n.70), kind=kLoop, calls=%fused_computation.30 | loop fusion | flops 524288 | bytes 2621444 | tf_op jit(solution)/shard_map/add | solution.py:51
  63.0 1.0 copy-done.1
  64.0 1.6 %collective-permute-start.3 = (bf16[256,512]{1,0:T(8,128)(2,1)S(1)}, bf16[256,512]{1,0:T(8,128)(2,1)S(1)}, u32[]{:S(2)}, u32[]{:S(2)}) collective-permute-start(bf16[256,512]{1,0:T(8,128)(2,1)S(1)} %fusion.23), channel_id=1, source_target_pairs={{0,16},{8,24},{16,0},{24,8},{1,17},{9,25},{17,1},{25,9},{2,18},{10... | collective-permute-start | bytes 786440 | tf_op jit(solution)/shard_map/ppermute | solution.py:51
  65.6 6.8 %collective-permute-done.3 = bf16[256,512]{1,0:T(8,128)(2,1)S(1)} collective-permute-done((bf16[256,512]{1,0:T(8,128)(2,1)S(1)}, bf16[256,512]{1,0:T(8,128)(2,1)S(1)}, u32[]{:S(2)}, u32[]{:S(2)}) %collective-permute-start.3) | collective-permute-done | bytes 262176 | tf_op jit(solution)/shard_map/ppermute | solution.py:51
  72.4 1.1 %fusion.15 = bf16[256,512]{1,0:T(8,128)(2,1)S(1)} fusion(bf16[256,512]{1,0:T(8,128)(2,1)S(1)} %collective-permute-done.3, f32[2,256,512]{2,1,0:T(8,128)} %bitcast.71, s32[]{:T(128)S(6)} %select_n.72), kind=kLoop, calls=%fused_computation.42 | loop fusion | flops 393216 | bytes 1048580 | tf_op jit(solution)/shard_map/convert_element_type | solution.py:52
  73.5 11.1 %all_to_all.25 = bf16[8,32,512]{2,1,0:T(8,128)(2,1)S(1)} all-to-all(bf16[8,32,512]{2,1,0:T(8,128)(2,1)S(1)} %bitcast.74), channel_id=1, replica_groups=mesh['group'=4,'dev'=8] {'dev'}, dimensions={0} | all-to-all | bytes 524288 | tf_op jit(solution)/shard_map/all_to_all | solution.py:41
  84.7 11.9 %all_to_all.26 = bf16[8,32,512]{2,1,0:T(8,128)(2,1)S(1)} all-to-all(bf16[8,32,512]{2,1,0:T(8,128)(2,1)S(1)} %broadcast_in_dim.32), channel_id=1, replica_groups=mesh['group'=4,'dev'=8] {'dev'}, dimensions={0} | all-to-all | bytes 524288 | tf_op jit(solution)/shard_map/all_to_all | solution.py:41
  96.6 1.5 %collective-permute-start.4 = (bf16[256,512]{1,0:T(8,128)(2,1)S(1)}, bf16[256,512]{1,0:T(8,128)(2,1)S(1)}, u32[]{:S(2)}, u32[]{:S(2)}) collective-permute-start(bf16[256,512]{1,0:T(8,128)(2,1)S(1)} %bitcast.73), channel_id=1, source_target_pairs={{0,16},{8,24},{16,0},{24,8},{1,17},{9,25},{17,1},{25,9},{2,18},{10... | collective-permute-start | bytes 786440 | tf_op jit(solution)/shard_map/ppermute | solution.py:29
  98.1 4.9 %collective-permute-done.4 = bf16[256,512]{1,0:T(8,128)(2,1)S(1)} collective-permute-done((bf16[256,512]{1,0:T(8,128)(2,1)S(1)}, bf16[256,512]{1,0:T(8,128)(2,1)S(1)}, u32[]{:S(2)}, u32[]{:S(2)}) %collective-permute-start.4) | collective-permute-done | bytes 262176 | tf_op jit(solution)/shard_map/ppermute | solution.py:29
  103.1 0.8 slice.131
  105.3 0.8 slice.141
  106.1 1.0 slice_bitcast_fusion
  107.2 0.8 pad_maximum_fusion.3
  (105 shorter events, 11.4 us)
Async XLA Ops:
  0.6 41.1 %copy-start = (bf16[512,512]{1,0:T(8,128)(2,1)S(1)}, bf16[512,512]{1,0:T(8,128)(2,1)}, u32[]{:S(2)}) copy-start(bf16[512,512]{1,0:T(8,128)(2,1)} %param.16) | copy-start | bytes 1572868
  2.3 10.2 %copy-start.8 = (s32[4096]{0:T(1024)S(1)}, s32[4096]{0:T(1024)}, u32[]{:S(2)}) copy-start(s32[4096]{0:T(1024)} %param.18) | copy-start | bytes 49156
  2.3 10.2 %copy-start.9 = (s32[4096]{0:T(1024)S(1)}, s32[4096]{0:T(1024)}, u32[]{:S(2)}) copy-start(s32[4096]{0:T(1024)} %param.19) | copy-start | bytes 49156
  2.3 10.2 %copy-start.13 = (s32[4096]{0:T(1024)S(1)}, s32[4096]{0:T(1024)}, u32[]{:S(2)}) copy-start(s32[4096]{0:T(1024)} %param.17) | copy-start | bytes 49156
  5.2 17.6 %all-to-all-start = ((bf16[8,40,512]{2,1,0:T(8,128)(2,1)}), bf16[8,40,512]{2,1,0:T(8,128)(2,1)S(1)}, u32[]{:S(2)}, u32[]{:S(2)}) async-start(bf16[8,40,512]{2,1,0:T(8,128)(2,1)} %pad_maximum_fusion.4), calls=%async_computation | async-start | bytes 655360 | tf_op jit(solution)/shard_map/all_to_all | solution.py:95
  12.5 10.3 %copy-start.7 = (bf16[512,256]{1,0:T(8,128)(2,1)S(1)}, bf16[512,256]{1,0:T(8,128)(2,1)}, u32[]{:S(2)}) copy-start(bf16[512,256]{1,0:T(8,128)(2,1)} %param.14) | copy-start | bytes 786436
  14.5 8.9 %copy-start.5 = (f32[320,320]{0,1:T(8,128)}, f32[320,320]{0,1:T(8,128)S(1)}, u32[]{:S(2)}) copy-start(f32[320,320]{0,1:T(8,128)S(1)} %get-tuple-element.16) | copy-start | bytes 1228804
  23.8 17.3 %copy-start.2 = (bf16[256,512]{1,0:T(8,128)(2,1)S(1)}, bf16[256,512]{1,0:T(8,128)(2,1)}, u32[]{:S(2)}) copy-start(bf16[256,512]{1,0:T(8,128)(2,1)} %param.15) | copy-start | bytes 786436
  24.5 11.4 %all-to-all-start.1 = ((bf16[8,48,256]{2,1,0:T(8,128)(2,1)}), bf16[8,48,256]{2,1,0:T(8,128)(2,1)S(1)}, u32[]{:S(2)}, u32[]{:S(2)}) async-start(bf16[8,48,256]{2,1,0:T(8,128)(2,1)} %fusion.33), calls=%async_computation.1 | async-start | bytes 393216 | tf_op jit(solution)/shard_map/all_to_all | solution.py:132
  36.0 1.2 %collective-permute-start = (f32[8,384]{1,0:T(8,128)S(1)}, f32[8,384]{1,0:T(8,128)S(1)}, u32[]{:S(2)}, u32[]{:S(2)}) collective-permute-start(f32[8,384]{1,0:T(8,128)S(1)} %pad_maximum_fusion.16), channel_id=1, source_target_pairs={{0,8},{8,0},{16,24},{24,16},{1,9},{9,1},{17,25},{25,17},{2,10},{10... | collective-permute-start | bytes 36872 | tf_op jit(solution)/shard_map/ppermute | solution.py:145
  36.3 5.1 %copy-start.10 = (bf16[8,512]{1,0:T(8,128)(2,1)S(1)}, bf16[8,512]{1,0:T(8,128)(2,1)}, u32[]{:S(2)}) copy-start(bf16[8,512]{1,0:T(8,128)(2,1)} %param.13) | copy-start | bytes 24580
  36.3 5.1 %copy-start.12 = (bf16[512,512]{1,0:T(8,128)(2,1)S(1)}, bf16[512,512]{1,0:T(8,128)(2,1)}, u32[]{:S(2)}) copy-start(bf16[512,512]{1,0:T(8,128)(2,1)} %param.12) | copy-start | bytes 1572868
  37.2 3.7 %collective-permute-start.1 = (f32[8,384]{1,0:T(8,128)S(1)}, f32[8,384]{1,0:T(8,128)S(1)}, u32[]{:S(2)}, u32[]{:S(2)}) collective-permute-start(f32[8,384]{1,0:T(8,128)S(1)} %fusion.60), channel_id=1, source_target_pairs={{0,16},{8,24},{16,0},{24,8},{1,17},{9,25},{17,1},{25,9},{2,18},{10... | collective-permute-start | bytes 36872 | tf_op jit(solution)/shard_map/ppermute | solution.py:145
  41.4 1.0 copy-start.11
  41.4 1.0 copy-start.14
  42.4 1.7 %copy-start.15 = (bf16[520,512]{1,0:T(8,128)(2,1)}, bf16[520,512]{1,0:T(8,128)(2,1)S(1)}, u32[]{:S(2)}) copy-start(bf16[520,512]{1,0:T(8,128)(2,1)S(1)} %fusion.5) | copy-start | bytes 1597444
  44.1 0.8 copy-start.17
  46.3 10.9 %all-to-all-start.2 = ((bf16[8,40,256]{2,1,0:T(8,128)(2,1)}), bf16[8,40,256]{2,1,0:T(8,128)(2,1)S(1)}, u32[]{:S(2)}, u32[]{:S(2)}) async-start(bf16[8,40,256]{2,1,0:T(8,128)(2,1)} %pad_maximum_fusion.9), calls=%async_computation.2 | async-start | bytes 327680 | tf_op jit(solution)/shard_map/all_to_all | solution.py:171
  50.3 1.0 copy-start.16
  50.3 1.2 %copy-start.18 = (bf16[520,512]{1,0:T(8,128)(2,1)S(1)}, bf16[520,512]{1,0:T(8,128)(2,1)}, u32[]{:S(2)}) copy-start(bf16[520,512]{1,0:T(8,128)(2,1)} %copy-done.17) | copy-start | bytes 1597444
  51.5 5.8 %copy-start.6 = (f32[320,320]{0,1:T(8,128)S(1)}, f32[320,320]{0,1:T(8,128)}, u32[]{:S(2)}) copy-start(f32[320,320]{0,1:T(8,128)} %copy-done.5) | copy-start | bytes 1228804
  58.1 1.2 %copy-start.3 = (f32[512,512]{1,0:T(8,128)S(1)}, f32[512,512]{1,0:T(8,128)}, u32[]{:S(2)}) copy-start(f32[512,512]{1,0:T(8,128)} %fusion.12) | copy-start | bytes 3145732
  59.6 2.1 %collective-permute-start.2 = (bf16[512,512]{1,0:T(8,128)(2,1)S(1)}, bf16[512,512]{1,0:T(8,128)(2,1)}, u32[]{:S(2)}, u32[]{:S(2)}) collective-permute-start(bf16[512,512]{1,0:T(8,128)(2,1)S(1)} %fusion.14), channel_id=1, source_target_pairs={{0,8},{8,0},{16,24},{24,16},{1,9},{9,1},{17,25},{25,17},{2,10},{10... | collective-permute-start | bytes 1572872 | tf_op jit(solution)/shard_map/ppermute | solution.py:51
  63.0 1.0 copy-start.1
  64.0 8.4 %collective-permute-start.3 = (bf16[256,512]{1,0:T(8,128)(2,1)S(1)}, bf16[256,512]{1,0:T(8,128)(2,1)S(1)}, u32[]{:S(2)}, u32[]{:S(2)}) collective-permute-start(bf16[256,512]{1,0:T(8,128)(2,1)S(1)} %fusion.23), channel_id=1, source_target_pairs={{0,16},{8,24},{16,0},{24,8},{1,17},{9,25},{17,1},{25,9},{2,18},{10... | collective-permute-start | bytes 786440 | tf_op jit(solution)/shard_map/ppermute | solution.py:51
  96.6 6.6 %copy-start.4 = (bf16[520,512]{1,0:T(8,128)(2,1)S(1)}, bf16[520,512]{1,0:T(8,128)(2,1)}, u32[]{:S(2)}) copy-start(bf16[520,512]{1,0:T(8,128)(2,1)} %get-tuple-element.8) | copy-start | bytes 1597444
  96.6 6.4 %collective-permute-start.4 = (bf16[256,512]{1,0:T(8,128)(2,1)S(1)}, bf16[256,512]{1,0:T(8,128)(2,1)S(1)}, u32[]{:S(2)}, u32[]{:S(2)}) collective-permute-start(bf16[256,512]{1,0:T(8,128)(2,1)S(1)} %bitcast.73), channel_id=1, source_target_pairs={{0,16},{8,24},{16,0},{24,8},{1,17},{9,25},{17,1},{25,9},{2,18},{10... | collective-permute-start | bytes 786440 | tf_op jit(solution)/shard_map/ppermute | solution.py:29
  103.0 2.0 %collective-permute-start.5 = (bf16[512,512]{1,0:T(8,128)(2,1)S(1)}, bf16[512,512]{1,0:T(8,128)(2,1)S(1)}, u32[]{:S(2)}, u32[]{:S(2)}) collective-permute-start(bf16[512,512]{1,0:T(8,128)(2,1)S(1)} %bitcast.72), channel_id=1, source_target_pairs={{0,8},{8,0},{16,24},{24,16},{1,9},{9,1},{17,25},{25,17},{2,10},{10... | collective-permute-start | bytes 1572872 | tf_op jit(solution)/shard_map/ppermute | solution.py:29
